TPU v7x, 32 devices: a whole 2x2x4 slice. The times are simulated.
32 devices in a mesh: ap: 8 (over z, x), ut: 4 (over y, core).
Axes of the slice: x: 2, y: 2, z: 4, core: 2. Of those that a mesh axis runs over, the one named last changes fastest.
Arguments:
- channel: bfloat16 [2, 2, 32, 64, 1024], P(None, None, 'ap', None, 'ut'), may hold values from -0.00390625 to 0.00390625
- start_precoder: bfloat16 [2, 2, 32, 64, 1024], P(None, None, 'ap', None, 'ut'), may hold values from -6 to 6
- cluster: int32 [32, 4], P('ap', 'ut'), may hold values 0 or 1
- noise: float32 [2, 1024], P(None, 'ut'), may hold values from 0.2 to 2
- penalty: float32 [32], P('ap'), may hold values from 2.3841858e-08 to 4.7683716e-07
- power: float32 [32], P('ap'), may hold values from 0.5 to 2
Outputs:
- precoder: bfloat16 [2, 2, 32, 64, 1024], P(None, None, 'ap', None, 'ut')
- user_weight: float32 [2, 1024], P(None, 'ut')
All inputs are finite; a program needn't handle non-finite values. No bound on the sum of `cluster` on one device may be relied on, other than what follows from the above.
Results may differ from a plain program's by a relative error of at most 0.003.
Values may be sent and summed in bfloat16 or wider, within the bound.
A program may use at most 64 MiB of HBM per device.

v0:
```python
import jax
import jax.numpy as jnp
from jax import lax
from jax.sharding import PartitionSpec as P


def masked_channel(channel, cluster):
    tile_users = channel.shape[-1] // cluster.shape[1]
    served = jnp.repeat(cluster, tile_users, axis=1).astype(jnp.bfloat16)
    return channel * served[None, None, :, None, :]


def stacked_rows(field):
    blocks, parts, points, antennas, users = field.shape
    return field.reshape(blocks, parts * points * antennas, users)


def partner(field):
    plain = stacked_rows(field)
    turned = stacked_rows(jnp.stack([field[:, 1], -field[:, 0]], axis=1))
    return jnp.stack([plain, turned], axis=1)


def user_terms(total, signal, noise):
    level = total + noise
    strength = signal[:, 0] * signal[:, 0] + signal[:, 1] * signal[:, 1]
    weight = level / (level - strength)
    filter_re = signal[:, 0] / level
    filter_im = signal[:, 1] / level
    coeff = weight * (filter_re * filter_re + filter_im * filter_im)
    return (weight, coeff, filter_re * weight, filter_im * weight)


def covariance(served, coeff):
    real_part = served[:, 0].astype(jnp.float32)
    imag_part = served[:, 1].astype(jnp.float32)
    first = jnp.concatenate([real_part, imag_part], axis=2)
    second = jnp.concatenate([-imag_part, real_part], axis=2)
    scaled = coeff[:, None, None, :]
    result = jnp.einsum("samk,sank->samn", first * scaled, first, precision=lax.Precision.HIGHEST)
    return result + jnp.einsum(
        "samk,sank->samn", second * scaled, second, precision=lax.Precision.HIGHEST
    )


def transmit_rhs(served, scaled_re, scaled_im):
    real_part = served[:, 0].astype(jnp.float32)
    imag_part = served[:, 1].astype(jnp.float32)
    weight_re = scaled_re[:, None, None, :]
    weight_im = scaled_im[:, None, None, :]
    out_re = real_part * weight_re - imag_part * weight_im
    out_im = real_part * weight_im + imag_part * weight_re
    return jnp.concatenate([out_re, out_im], axis=2)


def cholesky_solve(system, rhs):
    factor = jnp.linalg.cholesky(system)
    middle = lax.linalg.triangular_solve(factor, rhs, left_side=True, lower=True)
    return lax.linalg.triangular_solve(factor, middle, left_side=True, lower=True, transpose_a=True)


def split_field(raw):
    antennas = raw.shape[2] // 2
    return jnp.stack([raw[:, :, :antennas], raw[:, :, antennas:]], axis=1)


def own_signal(served, precoder):
    chan_re = served[:, 0].astype(jnp.float32)
    chan_im = served[:, 1].astype(jnp.float32)
    prec_re = precoder[:, 0].astype(jnp.float32)
    prec_im = precoder[:, 1].astype(jnp.float32)
    signal_re = jnp.sum(chan_re * prec_re + chan_im * prec_im, axis=(1, 2))
    signal_im = jnp.sum(chan_re * prec_im - chan_im * prec_re, axis=(1, 2))
    return jnp.stack([signal_re, signal_im], axis=1)


def local(channel, start_precoder, cluster, noise, penalty, power):
    served = masked_channel(channel, cluster)
    rows = stacked_rows(served)
    user_count = channel.shape[-1]
    antennas = channel.shape[3]
    all_users = user_count * lax.axis_size("ut")
    ident = jnp.eye(2 * antennas, dtype=jnp.float32)
    precoder = start_precoder
    gain = jnp.einsum(
        "srk,scrj->sckj",
        rows,
        partner(lax.all_gather(precoder, "ut", axis=4, tiled=True)),
        preferred_element_type=jnp.float32,
    )
    portion = lax.psum_scatter(
        gain.astype(jnp.bfloat16), "ap", scatter_dimension=3, tiled=True
    ).astype(jnp.float32)
    local_total = jnp.sum(portion * portion, axis=(1, 3))
    local_signal = own_signal(served, precoder)
    total, signal = lax.psum((local_total, local_signal), "ap")
    weight, coeff, scaled_re, scaled_im = user_terms(total, signal, noise)
    partial_cov = covariance(served, coeff)
    rhs = transmit_rhs(served, scaled_re, scaled_im)
    summed = lax.psum(partial_cov, "ut")
    system = summed + penalty[None, :, None, None] * ident
    raw = cholesky_solve(system, rhs)
    field = split_field(raw)
    local_power = jnp.sum(field * field, axis=(0, 1, 3, 4))
    summed_power = lax.psum(local_power, "ut")
    mean_sq = summed_power / (2.0 * field.shape[0] * antennas * all_users)
    factor = jnp.sqrt(power / (mean_sq + 1e-06))
    precoder = (field * factor[None, None, :, None, None]).astype(jnp.bfloat16)
    return (precoder, weight)


def solution(mesh):
    in_specs = (
        P(None, None, "ap", None, "ut"),
        P(None, None, "ap", None, "ut"),
        P("ap", "ut"),
        P(None, "ut"),
        P("ap"),
        P("ap"),
    )
    out_specs = (P(None, None, "ap", None, "ut"), P(None, "ut"))
    return jax.shard_map(local, mesh=mesh, in_specs=in_specs, out_specs=out_specs, check_vma=False)
```

profile of v0, /device:TPU:0, one launch (start us, length us, event | category | flops | bytes accessed | tf_op | source)
XLA Modules:
  0.0 362.5 jit_solution(17723871569002901044)
XLA Ops:
  7.2 0.7 all-gather.2.cloned.1.call-update
  7.9 0.7 convert_bitcast_fusion.1
  8.6 1.1 copy_multiply_fusion
  9.8 25.3 %all-gather.2.cloned.1.call-done = bf16[2,2,4,64,1024]{4,3,2,1,0:T(8,128)(2,1)} async-done(((bf16[2,2,4,64,256]{4,3,2,1,0:T(8,128)(2,1)}), bf16[2,2,4,64,1024]{4,3,2,1,0:T(8,128)(2,1)}) %all-gather.2.cloned.1.call-update) | async-done | bytes 2097168 | tf_op jit(solution)/shard_map/all_gather | solution.py:88
  35.1 1.7 fusion.47
  36.8 1.5 pad_maximum_fusion
  38.3 4.1 %copy.31 = bf16[2,1,512,1024]{2,3,1,0:T(8,128)(2,1)} copy(bf16[2,1,512,1024]{3,2,0,1:T(8,128)(2,1)} %bitcast.87) | data formatting | bytes 4194304 | tf_op jit(solution)/shard_map/stack;reshape | solution.py:21
  42.4 2.6 copy.30
  45.0 4.8 %convert_bitcast_fusion = bf16[2,2,256,1024]{2,3,1,0:T(8,128)(2,1)} fusion(bf16[2,512,256,1]{2,1,3,0:T(8,128)(2,1)S(1)} %bitcast.88, bf16[2,1,512,1024]{2,3,1,0:T(8,128)(2,1)} %copy.31, bf16[2,1,512,1024]{2,3,1,0:T(8,128)(2,1)} %copy.30), kind=kOutput, calls=%fused_computation.5 | convolution fusion | flops 1076887552 | bytes 6815744 | tf_op jit(solution)/shard_map/srk,scrj->sckj/dot_general | solution.py:85
  49.8 1.0 copy-done.2
  50.8 0.2 fusion.26
  51.2 66.7 %reduce-scatter.2.cloned.1.call-done = bf16[2,2,256,128]{2,3,1,0:T(8,128)(2,1)} async-done(((bf16[2,2,256,1024]{2,3,1,0:T(8,128)(2,1)}), bf16[2,2,256,128]{2,3,1,0:T(8,128)(2,1)}) %reduce-scatter.2.cloned.1.call-update) | async-done | bytes 262160 | tf_op jit(solution)/shard_map/reduce_scatter | solution.py:91
  117.9 1.0 multiply_reduce_fusion.1
  118.9 19.6 %all-reduce = (f32[2,2,256]{2,0,1:T(2,128)S(1)}, f32[2,256]{1,0:T(2,128)S(1)}) all-reduce(f32[2,2,256]{2,0,1:T(2,128)S(1)} %pad_maximum_fusion.2, f32[2,256]{1,0:T(2,128)S(1)} %multiply_reduce_fusion.1), channel_id=1, replica_groups=mesh['ap'=8,'ut'=4] {'ap'}, use_global_device_ids=true, to_apply=%region_5.0 | all-reduce | flops 1536 | bytes 12288 | tf_op jit(solution)/shard_map/psum | solution.py:96
  138.7 1.2 fusion.6
  140.0 2.0 fusion.10
  142.2 30.4 %all-reduce.3.cloned.1.call-done = f32[2,4,128,128]{2,3,1,0:T(8,128)} async-done(((f32[2,4,128,128]{2,3,1,0:T(8,128)}), f32[2,4,128,128]{2,3,1,0:T(8,128)}) %all-reduce.3.cloned.1.call-update) | async-done | bytes 524304 | tf_op jit(solution)/shard_map/psum | solution.py:100
  172.6 1.2 broadcast_add_fusion
  174.0 93.8 %custom-call.9 = f32[2,4,128,128]{3,2,1,0:T(8,128)S(1)} custom-call(f32[2,4,128,128]{3,2,1,0:T(8,128)S(1)} %fusion.32), custom_call_target="Cholesky" | custom-call | tf_op jit(solution)/shard_map/jit(cholesky)/cholesky | solution.py:57
  268.2 78.6 %custom-call.10 = f32[2,4,1,128,128]{3,4,2,1,0:T(8,128)S(1)} custom-call(f32[2,4,1,128,128]{4,3,2,1,0:T(8,128)S(1)} %select_bitcast_fusion), custom_call_target="InvertDiagBlocksLowerTriangular" | custom-call | tf_op jit(solution)/shard_map/triangular_solve | solution.py:59
  346.8 1.0 fusion.19
  347.9 1.0 fusion.29
  349.2 5.7 %psum.31 = f32[4]{0:T(128)S(1)} all-reduce(f32[4]{0:T(128)S(1)} %multiply_reduce_fusion), channel_id=1, replica_groups=mesh['ap'=8,'ut'=4] {'ut'}, use_global_device_ids=true, to_apply=%region_10.11 | all-reduce | flops 4 | bytes 32 | tf_op jit(solution)/shard_map/psum | solution.py:105
  355.1 0.8 copy.40
  (38 shorter events, 1.8 us)
Async XLA Ops:
  7.2 28.0 %all-gather.2.cloned.1.call-start = ((), (), s32[]{:S(2)}) async-start(), calls=%async_computation.1 | async-start | bytes 2621440 | tf_op jit(solution)/shard_map/all_gather | solution.py:88
  7.9 110.0 %reduce-scatter.2.cloned.1.call-start = ((), (), s32[]{:S(2)}) async-start(), calls=%async_computation.2 | async-start | bytes 2359296 | tf_op jit(solution)/shard_map/reduce_scatter | solution.py:91
  38.3 4.1 %copy-start = (bf16[2,2,4,64,1024]{4,3,2,1,0:T(8,128)(2,1)S(1)}, bf16[2,2,4,64,1024]{4,3,2,1,0:T(8,128)(2,1)}, u32[]{:S(2)}) copy-start(bf16[2,2,4,64,1024]{4,3,2,1,0:T(8,128)(2,1)} %all-gather.2.cloned.1.call-done) | copy-start | bytes 6291460
  49.8 1.0 copy-start.2
  49.8 88.7 %copy-start.4 = (f32[2,256]{1,0:T(2,128)S(1)}, f32[2,256]{1,0:T(2,128)}, u32[]{:S(2)}) copy-start(f32[2,256]{1,0:T(2,128)} %param.9) | copy-start | bytes 6148
  49.8 122.8 %all-reduce.3.cloned.1.call-start = ((), (), s32[]{:S(2)}) async-start(), calls=%async_computation.3 | async-start | bytes 1048576 | tf_op jit(solution)/shard_map/psum | solution.py:100
  138.5 1.4 copy-start.3
  139.9 2.2 copy-start.5
  172.6 1.4 copy-start.1
  348.9 6.0 %copy-start.6 = (f32[4]{0:T(128)S(1)}, f32[4]{0:T(128)}, u32[]{:S(2)}) copy-start(f32[4]{0:T(128)} %param.11) | copy-start | bytes 52
Sparse Core Ops, SparseCore 0:
  9.5 25.5 all-gather.1
  49.9 67.9 reduce-scatter.1
  142.1 30.4 all-reduce.2
where the time goes:
time: 363 us; the launch traced here: 362 us
  other arithmetic  181 us (50%)
  waiting for transfers between devices  123 us (34%)
  blocking collectives  25.3 us (7%)
  between operations  14 us (4%)
  matrix products  10 us (3%)
  local copies, waits for them, and re-layouts  8.92 us (2%)
    another operation x4, other arithmetic, cholesky_solve(): factor = jnp.linalg.cholesky(system)  94 us
    another operation x3, other arithmetic, cholesky_solve(): lax.linalg.triangular_solve(factor, middle, left_side=True, lower=True, t...  78.8 us
    reduce_scatter x1, waiting for transfers between devices, local(): lax.psum_scatter(gain.astype(jnp.bfloat16), 'ap', scatter_dimension=3, ti...  66.7 us
    psum x1, waiting for transfers between devices, local(): summed = lax.psum(partial_cov, 'ut')  30.4 us
    all_gather x1, waiting for transfers between devices, local(): lax.all_gather(precoder, 'ut', axis=4, tiled=True)  25.3 us
    psum x1, blocking collectives, local(): total, signal = lax.psum((local_total, local_signal), 'ap')  19.6 us
  transfers between devices with their start and end apart: 3, of which 3 were waited for; matrix products, arithmetic and copies ran while one was open for 1% of the time, Pallas kernels for 0%

commit v1 on v0

v1 whole, which is shorter than its diff:
```python
import functools
import jax
import jax.numpy as jnp
from jax import lax
from jax.experimental import pallas as pl
from jax.experimental.pallas import tpu as pltpu
from jax.sharding import PartitionSpec as P

MESH = pl.DeviceIdType.MESH
F32 = jnp.float32
BF16 = jnp.bfloat16


def low_bit(mask):
    return mask & -mask


def three_parts(value):
    first = value.astype(BF16)
    rest = value - first.astype(F32)
    second = rest.astype(BF16)
    third = (rest - second.astype(F32)).astype(BF16)
    return first, second, third


def kernel(
    n_ap, n_ut, bits, width, chan, prec, clus, noise, penalty, power,
    out, weight_out,
    vbuf, lhs, pair, send, recv, keep, square, msgs, covs, cov_in, work, invs, raw, pows,
    v_send, v_recv, g_send, g_recv, t_send, t_recv, c_send, c_recv, i_send, i_recv, p_send, p_recv,
):
    blocks, parts, points, antennas, users = chan.shape
    rows = points * antennas
    halves = users // width
    per = covs.shape[1]
    ap = lax.axis_index("ap")
    ut = lax.axis_index("ut")

    def ap_peer(step):
        return (lax.rem(ap + step, n_ap), ut)

    def ap_flip(bit):
        return (ap + (1 << bit) - 2 * (1 << bit) * (lax.div(ap, 1 << bit) % 2), ut)

    def ut_flip_index(mask):
        index = ut
        bit = 1
        while bit <= mask:
            if mask & bit:
                index = index + bit - 2 * bit * (lax.div(ut, bit) % 2)
            bit *= 2
        return index

    def ut_flip(mask):
        return (ap, ut_flip_index(mask))

    barrier = pltpu.get_barrier_semaphore()
    for step in range(1, n_ap):
        pl.semaphore_signal(barrier, inc=1, device_id=ap_peer(step), device_id_type=MESH)
    for mask in range(1, n_ut):
        pl.semaphore_signal(barrier, inc=1, device_id=ut_flip(mask), device_id_type=MESH)
    pl.semaphore_wait(barrier, n_ap + n_ut - 2)

    pending = []

    def lanes(half):
        return pl.ds(half * width, width)

    def v_copy(mask, half):
        source = mask ^ low_bit(mask)
        if source == 0:
            src = prec.at[:, :, :, :, lanes(half)]
        else:
            src = vbuf.at[source - 1, :, :, :, :, lanes(half)]
        return pltpu.make_async_remote_copy(
            src_ref=src,
            dst_ref=vbuf.at[mask - 1, :, :, :, :, lanes(half)],
            send_sem=v_send.at[mask - 1, half],
            recv_sem=v_recv.at[mask - 1, half],
            device_id=ut_flip(low_bit(mask)),
            device_id_type=MESH,
        )

    def v_start(mask, half):
        copy = v_copy(mask, half)
        copy.start()
        pending.append(copy)

    singles = [m for m in range(n_ut - 1, 0, -1) if m == low_bit(m)]
    for half in range(halves):
        for mask in singles:
            v_start(mask, half)

    def v_arrived(mask, half):
        v_copy(mask, half).wait_recv()
        for later in range(n_ut):
            if later != low_bit(later) and (later ^ low_bit(later)) == mask:
                v_start(later, half)

    tile_users = users // clus.shape[1]
    for s in range(blocks):
        turned = []
        for part in range(parts):
            point_rows = []
            for a in range(points):
                value = chan[s, part, a].astype(F32)
                cut = [
                    value[:, c * tile_users:(c + 1) * tile_users] * clus[a, c].astype(F32)
                    for c in range(clus.shape[1])
                ]
                value = cut[0] if len(cut) == 1 else jnp.concatenate(cut, axis=1)
                point_rows.append(value)
                here = slice(part * antennas, (part + 1) * antennas)
                there = slice((1 - part) * antennas, (2 - part) * antennas)
                pair[s, a, here, 0:users] = value.astype(BF16)
                pair[s, a, there, users:2 * users] = (value if part == 0 else -value).astype(BF16)
            turned.append(jnp.concatenate(point_rows, axis=0).T)
        lhs[s, 0:users, 0:rows] = turned[0].astype(BF16)
        lhs[s, 0:users, rows:2 * rows] = turned[1].astype(BF16)
        lhs[s, users:2 * users, 0:rows] = (-turned[1]).astype(BF16)
        lhs[s, users:2 * users, rows:2 * rows] = turned[0].astype(BF16)

    all_rows = blocks * 2 * users
    own_bit = [lax.div(ap, 1 << b) % 2 for b in range(bits)]

    def g_copy(level, c):
        return pltpu.make_async_remote_copy(
            src_ref=send[level].at[c],
            dst_ref=recv[level].at[c],
            send_sem=g_send.at[level, c],
            recv_sem=g_recv.at[level, c],
            device_id=ap_flip(level),
            device_id_type=MESH,
        )

    def g_start(level, c):
        copy = g_copy(level, c)
        copy.start()
        pending.append(copy)

    some = blocks // 2

    def gains(s, slot, half):
        ref = prec if slot == 0 else vbuf.at[slot - 1]
        field = ref[s, :, :, :, half * width:(half + 1) * width].reshape(2 * rows, width)
        return jnp.dot(lhs[s], field, preferred_element_type=F32)

    def first_stage(c):
        slot, half = chunks[c]
        if slot:
            v_arrived(slot, half)
        for i in range(some):
            value = gains((1 - own_bit[0]) * some + i, slot, half)
            send[0][c, i * 2 * users:(i + 1) * 2 * users] = value.astype(BF16)
        g_start(0, c)
        for i in range(some):
            keep[0][c, i * 2 * users:(i + 1) * 2 * users] = gains(own_bit[0] * some + i, slot, half)

    def next_stage(level, c):
        g_copy(level - 1, c).wait_recv()
        if level == bits:
            total = keep[level - 1][c] + recv[level - 1][c].astype(F32)
            square[...] = total * total if c == 0 else square[...] + total * total
            return
        size = all_rows >> (level + 1)
        away = pl.ds(pl.multiple_of((1 - own_bit[level]) * size, size), size)
        mine = pl.ds(pl.multiple_of(own_bit[level] * size, size), size)
        send[level][c] = (keep[level - 1][c, away] + recv[level - 1][c, away].astype(F32)).astype(BF16)
        g_start(level, c)
        keep[level][c] = keep[level - 1][c, mine] + recv[level - 1][c, mine].astype(F32)

    chunks = [(slot, half) for slot in range(min(2, n_ut)) for half in range(halves)]
    lead = len(chunks)
    chunks += [(slot, half) for half in range(halves) for slot in range(2, n_ut)]
    count = len(chunks)
    for c in range(lead):
        first_stage(c)

    for s in range(blocks):
        sums = [jnp.zeros((1, users), F32), jnp.zeros((1, users), F32)]
        for a in range(points):
            hr = pair[s, a, 0:antennas, 0:users].astype(F32)
            hi = pair[s, a, antennas:2 * antennas, 0:users].astype(F32)
            vr = prec[s, 0, a].astype(F32)
            vi = prec[s, 1, a].astype(F32)
            sums[0] = sums[0] + jnp.sum(hr * vr + hi * vi, axis=0, keepdims=True)
            sums[1] = sums[1] + jnp.sum(hr * vi - hi * vr, axis=0, keepdims=True)
        for part in range(2):
            msgs[ap, blocks * (1 + part) + s:blocks * (1 + part) + s + 1] = sums[part]

    for i in range(count + bits - 1):
        for level in range(1, bits + 1):
            c = i - (level - 1)
            if 0 <= c < count:
                next_stage(level, c)
        if lead + i < count:
            first_stage(lead + i)

    held = all_rows >> bits
    offset = own_bit[0] * (all_rows // 2)
    for b in range(1, bits):
        offset = offset + own_bit[b] * (all_rows >> (b + 1))
    own_block = lax.div(offset, 2 * users)
    first_user = lax.rem(offset, users)
    column = jnp.sum(square[...], axis=1, keepdims=True)
    diagonal = (
        lax.broadcasted_iota(jnp.int32, (held, users), 1)
        == lax.broadcasted_iota(jnp.int32, (held, users), 0) + first_user
    )
    spread = jnp.sum(jnp.where(diagonal, column, 0.0), axis=0, keepdims=True)
    place = lax.broadcasted_iota(jnp.int32, (blocks, users), 0) == own_block
    msgs[ap, 0:blocks] = jnp.where(place, spread, 0.0)

    t_copies = [
        pltpu.make_async_remote_copy(
            src_ref=msgs.at[ap],
            dst_ref=msgs.at[ap],
            send_sem=t_send.at[step - 1],
            recv_sem=t_recv.at[step - 1],
            device_id=ap_peer(step),
            device_id_type=MESH,
        )
        for step in range(1, n_ap)
    ]
    for copy in t_copies:
        copy.start()
    for copy in t_copies:
        copy.wait_recv()
    sums = msgs[0]
    for q in range(1, n_ap):
        sums = sums + msgs[q]
    total = sums[0:blocks]
    signal_re = sums[blocks:2 * blocks]
    signal_im = sums[2 * blocks:3 * blocks]
    level = total + noise[...]
    strength = signal_re * signal_re + signal_im * signal_im
    weight = level / (level - strength)
    filter_re = signal_re / level
    filter_im = signal_im / level
    coeff = weight * (filter_re * filter_re + filter_im * filter_im)
    scaled_re = filter_re * weight
    scaled_im = filter_im * weight
    weight_out[...] = weight

    for s in range(blocks):
        for a in range(points):
            index = s * points + a
            both = pair[s, a]
            scale = coeff[s:s + 1]
            top = jnp.concatenate(
                [both[0:antennas, 0:users].astype(F32) * scale,
                 both[0:antennas, users:2 * users].astype(F32) * scale], axis=1)
            value = None
            for piece in reversed(three_parts(top)):
                term = lax.dot_general(
                    piece, both, (((1,), (1,)), ((), ())), preferred_element_type=F32)
                value = term if value is None else value + term
            covs[index // per, index % per] = value
    c_copies = [
        pltpu.make_async_remote_copy(
            src_ref=covs.at[ut_flip_index(mask)],
            dst_ref=cov_in.at[mask - 1],
            send_sem=c_send.at[mask - 1],
            recv_sem=c_recv.at[mask - 1],
            device_id=ut_flip(mask),
            device_id_type=MESH,
        )
        for mask in range(n_ut - 1, 0, -1)
    ]
    for copy in c_copies:
        copy.start()
    for copy in c_copies:
        copy.wait_recv()

    shape = (antennas, 2 * antennas)
    row_of = lax.broadcasted_iota(jnp.int32, shape, 0)
    lane_of = lax.broadcasted_iota(jnp.int32, shape, 1)
    lane_row = lane_of[0:1]
    for p in range(per):
        value = covs[ut, p]
        for mask in range(1, n_ut):
            value = value + cov_in[mask - 1, p]
        load = penalty[lax.rem(ut * per + p, points)]
        work[p] = value + jnp.where(row_of == lane_of, load, 0.0)

    sign = jnp.where(lane_row < antennas, -1.0, 1.0).astype(F32)

    def sweep(k, carry):
        is_row = row_of == k
        at_re = lane_of == k
        at_im = lane_of == k + antennas
        clear = is_row | at_re | at_im
        for p in range(per):
            value = work[p]
            row = work[p, pl.ds(k, 1)]
            pivot = jnp.sum(jnp.where(lane_row == k, row, 0.0), axis=1, keepdims=True)
            inverse = 1.0 / pivot
            col_re = jnp.sum(jnp.where(at_re, value, 0.0), axis=1, keepdims=True)
            col_im = jnp.sum(jnp.where(at_im, value, 0.0), axis=1, keepdims=True)
            row = jnp.where(lane_row == k, -inverse, jnp.where(lane_row == k + antennas, 0.0, row * inverse))
            turned = pltpu.roll(row, antennas, 1) * sign
            col_re = jnp.where(is_row, -1.0, col_re)
            col_im = jnp.where(is_row, 0.0, col_im)
            work[p] = jnp.where(clear, 0.0, value) - (col_re * row + col_im * turned)
        return carry

    lax.fori_loop(0, antennas, sweep, 0)
    for p in range(per):
        invs[ut, p] = -work[p]

    i_copies = [
        pltpu.make_async_remote_copy(
            src_ref=invs.at[ut],
            dst_ref=invs.at[ut],
            send_sem=i_send.at[mask - 1],
            recv_sem=i_recv.at[mask - 1],
            device_id=ut_flip(mask),
            device_id_type=MESH,
        )
        for mask in range(n_ut - 1, 0, -1)
    ]
    for copy in i_copies:
        copy.start()
    for copy in i_copies:
        copy.wait_recv()

    for a in range(points):
        power_row = jnp.zeros((1, users), F32)
        for s in range(blocks):
            index = s * points + a
            value = None
            for piece in reversed(three_parts(invs[index // per, index % per])):
                term = jnp.dot(piece, pair[s, a], preferred_element_type=F32)
                value = term if value is None else value + term
            base_re = value[:, 0:users]
            base_im = -value[:, users:2 * users]
            raw_re = base_re * scaled_re[s:s + 1] - base_im * scaled_im[s:s + 1]
            raw_im = base_re * scaled_im[s:s + 1] + base_im * scaled_re[s:s + 1]
            raw[s, 0, a] = raw_re
            raw[s, 1, a] = raw_im
            power_row = power_row + jnp.sum(raw_re * raw_re + raw_im * raw_im, axis=0, keepdims=True)
        pows[ut, a:a + 1] = power_row
    p_copies = [
        pltpu.make_async_remote_copy(
            src_ref=pows.at[ut],
            dst_ref=pows.at[ut],
            send_sem=p_send.at[mask - 1],
            recv_sem=p_recv.at[mask - 1],
            device_id=ut_flip(mask),
            device_id_type=MESH,
        )
        for mask in range(n_ut - 1, 0, -1)
    ]
    for copy in p_copies:
        copy.start()
    for copy in p_copies:
        copy.wait_recv()
    sums = pows[0]
    for q in range(1, n_ut):
        sums = sums + pows[q]
    mean = jnp.sum(sums, axis=1, keepdims=True) / (2.0 * blocks * antennas * users * n_ut)
    for a in range(points):
        factor = jnp.sqrt(power[a] / (mean[a:a + 1] + 1e-06))
        for s in range(blocks):
            for part in range(2):
                out[s, part, a] = (raw[s, part, a] * factor).astype(BF16)

    for copy in pending + t_copies + c_copies + i_copies + p_copies:
        copy.wait_send()


def local(n_ap, n_ut, channel, start_precoder, cluster, noise, penalty, power):
    blocks, parts, points, antennas, users = channel.shape
    bits = n_ap.bit_length() - 1
    width = 128 if users % 128 == 0 else users
    halves = users // width
    count = n_ut * halves
    rows = points * antennas
    per = blocks * points // n_ut
    all_rows = blocks * 2 * users
    sizes = [all_rows >> (b + 1) for b in range(bits)]
    vmem = pl.BlockSpec(memory_space=pltpu.VMEM)
    smem = pl.BlockSpec(memory_space=pltpu.SMEM)
    dma = pltpu.SemaphoreType.DMA
    return pl.pallas_call(
        functools.partial(kernel, n_ap, n_ut, bits, width),
        out_shape=(
            jax.ShapeDtypeStruct(channel.shape, BF16),
            jax.ShapeDtypeStruct((blocks, users), F32),
        ),
        in_specs=[vmem, vmem, smem, vmem, smem, smem],
        out_specs=(vmem, vmem),
        scratch_shapes=[
            pltpu.VMEM((n_ut - 1,) + channel.shape, BF16),
            pltpu.VMEM((blocks, 2 * users, 2 * rows), BF16),
            pltpu.VMEM((blocks, points, 2 * antennas, 2 * users), BF16),
            [pltpu.VMEM((count, size, width), BF16) for size in sizes],
            [pltpu.VMEM((count, size, width), BF16) for size in sizes],
            [pltpu.VMEM((count, size, width), F32) for size in sizes],
            pltpu.VMEM((all_rows >> bits, width), F32),
            pltpu.VMEM((n_ap, 3 * blocks, users), F32),
            pltpu.VMEM((n_ut, per, antennas, 2 * antennas), F32),
            pltpu.VMEM((n_ut - 1, per, antennas, 2 * antennas), F32),
            pltpu.VMEM((per, antennas, 2 * antennas), F32),
            pltpu.VMEM((n_ut, per, antennas, 2 * antennas), F32),
            pltpu.VMEM(channel.shape, F32),
            pltpu.VMEM((n_ut, points, users), F32),
            dma((n_ut - 1, halves)),
            dma((n_ut - 1, halves)),
            dma((bits, count)),
            dma((bits, count)),
            dma((n_ap - 1,)),
            dma((n_ap - 1,)),
            dma((n_ut - 1,)),
            dma((n_ut - 1,)),
            dma((n_ut - 1,)),
            dma((n_ut - 1,)),
            dma((n_ut - 1,)),
            dma((n_ut - 1,)),
        ],
        compiler_params=pltpu.CompilerParams(
            collective_id=0, has_side_effects=True, vmem_limit_bytes=40 * 1024 * 1024
        ),
    )(channel, start_precoder, cluster, noise, penalty, power)


def solution(mesh):
    in_specs = (
        P(None, None, "ap", None, "ut"),
        P(None, None, "ap", None, "ut"),
        P("ap", "ut"),
        P(None, "ut"),
        P("ap"),
        P("ap"),
    )
    out_specs = (P(None, None, "ap", None, "ut"), P(None, "ut"))
    body = functools.partial(local, mesh.shape["ap"], mesh.shape["ut"])
    return jax.shard_map(body, mesh=mesh, in_specs=in_specs, out_specs=out_specs, check_vma=False)
```

time: 363 us -> 83.5 us (0.23)
  other arithmetic: 181 us -> 0 us
  waiting for transfers between devices: 123 us -> 0 us
  Pallas kernels: 0 us -> 77.7 us
  blocking collectives: 25.3 us -> 0 us
  between operations: 14 us -> 0.66 us
  matrix products: 10 us -> 0 us
  local copies, waits for them, and re-layouts: 8.92 us -> 4.87 us
    another operation x9 -> x0, other arithmetic: 174 us -> none  [the longest x4 94 us: cholesky_solve(): factor = jnp.linalg.cholesky(system)]
    pallas_call x0 -> x1, Pallas kernels: none -> 77.7 us  [local(): pl.pallas_call(functools.partial(kernel, n_ap, n_ut, bits, width), out_sh...]
    reduce_scatter x1 -> x0, waiting for transfers between devices: 66.7 us -> none  [local(): lax.psum_scatter(gain.astype(jnp.bfloat16), 'ap', scatter_dimension=3, ti...]
    psum x1 -> x0, waiting for transfers between devices: 30.4 us -> none  [local(): summed = lax.psum(partial_cov, 'ut')]
    all_gather x1 -> x0, waiting for transfers between devices: 25.3 us -> none  [local(): lax.all_gather(precoder, 'ut', axis=4, tiled=True)]
    psum x2 -> x0, blocking collectives: 25.3 us -> none  [the longest x1 19.6 us: local(): total, signal = lax.psum((local_total, local_signal), 'ap')]
    dot_general x3 -> x0, matrix products: 7.97 us -> none  [the longest x1 4.77 us: local(): jnp.einsum('srk,scrj->sckj', rows, partner(lax.all_gather(precoder, 'ut',...]
    another operation x3 -> x0, local copies, waits for them, and re-layouts: 6.76 us -> none  [the longest x2 6.67 us: partner(): return jnp.stack([plain, turned], axis=1)]
  transfers between devices with their start and end apart: 3 -> 0, of which waited for: 3 -> 0; matrix products, arithmetic and copies ran while one was open for 1% -> 0% of each run, Pallas kernels for 0% -> 0%
where the time goes in v1:
time: 83.5 us; the launch traced here: 83.2 us
  Pallas kernels  77.7 us (93%)
  local copies, waits for them, and re-layouts  4.87 us (6%)
    pallas_call x1, Pallas kernels, local(): pl.pallas_call(functools.partial(kernel, n_ap, n_ut, bits, width), out_sh...  77.7 us
    unnamed x13, local copies, waits for them, and re-layouts  4.87 us

profile of v1, /device:TPU:0, one launch (start us, length us, event | category | flops | bytes accessed | tf_op | source)
XLA Modules:
  0.0 83.2 jit_solution(6333671864966451472)
XLA Ops:
  0.6 0.0 copy-start.3
  0.6 0.0 copy-start.2
  0.7 0.8 copy.8.clus
  1.4 0.0 copy-done.3
  1.4 0.0 copy-done.2
  1.4 0.0 copy-start
  1.4 1.0 %copy-done = bf16[2,2,4,64,256]{4,3,2,1,0:T(8,128)(2,1)S(1)} copy-done((bf16[2,2,4,64,256]{4,3,2,1,0:T(8,128)(2,1)S(1)}, bf16[2,2,4,64,256]{4,3,2,1,0:T(8,128)(2,1)}, u32[]{:S(2)}) %copy-start) | copy-done | bytes 524312
  2.5 0.0 copy-start.1
  2.5 1.0 %copy-done.1 = bf16[2,2,4,64,256]{4,3,2,1,0:T(8,128)(2,1)S(1)} copy-done((bf16[2,2,4,64,256]{4,3,2,1,0:T(8,128)(2,1)S(1)}, bf16[2,2,4,64,256]{4,3,2,1,0:T(8,128)(2,1)}, u32[]{:S(2)}) %copy-start.1) | copy-done | bytes 524312
  3.5 0.0 copy-start.4
  3.5 0.7 copy-done.4
  4.2 77.7 %shard_map.77 = (bf16[2,2,4,64,256]{4,3,2,1,0:T(8,128)(2,1)S(1)}, f32[2,256]{1,0:T(2,128)S(1)}) custom-call(bf16[2,2,4,64,256]{4,3,2,1,0:T(8,128)(2,1)S(1)} %copy-done, bf16[2,2,4,64,256]{4,3,2,1,0:T(8,128)(2,1)S(1)} %copy-done.1, s32[4,1]{1,0:T(4,128)S(1)} %copy.8.clus, f32[2,256]{1,0:T(2,128)S(1)} %copy-done.2, f32[4]{0:T(128)S(1)} %copy-done.3, ...), custom_call_target="tpu_custom_call" | custom-call | tf_op jit(solution)/shard_map/pallas_call | solution.py:385
  81.8 0.8 copy.11
  82.6 0.6 copy.12
Async XLA Ops:
  0.6 0.8 copy-start.3
  0.6 0.8 copy-start.2
  1.4 1.0 %copy-start = (bf16[2,2,4,64,256]{4,3,2,1,0:T(8,128)(2,1)S(1)}, bf16[2,2,4,64,256]{4,3,2,1,0:T(8,128)(2,1)}, u32[]{:S(2)}) copy-start(bf16[2,2,4,64,256]{4,3,2,1,0:T(8,128)(2,1)} %chan.1) | copy-start | bytes 1572868
  2.5 1.0 %copy-start.1 = (bf16[2,2,4,64,256]{4,3,2,1,0:T(8,128)(2,1)S(1)}, bf16[2,2,4,64,256]{4,3,2,1,0:T(8,128)(2,1)}, u32[]{:S(2)}) copy-start(bf16[2,2,4,64,256]{4,3,2,1,0:T(8,128)(2,1)} %prec.1) | copy-start | bytes 1572868
  3.5 0.7 copy-start.4

commit v2 on v1

--- a/solution.py
+++ b/solution.py
@@ -24,9 +24,9 @@
 
 
 def kernel(
-    n_ap, n_ut, bits, width, chan, prec, clus, noise, penalty, power,
+    n_ap, n_ut, bits, width, chan_in, prec_in, clus, noise_in, penalty, power,
     out, weight_out,
-    vbuf, lhs, pair, send, recv, keep, square, msgs, covs, cov_in, work, invs, raw, pows,
+    chan, noise, fetch, vbuf, lhs, pair, send, recv, keep, square, msgs, covs, cov_in, work, invs, raw, pows,
     v_send, v_recv, g_send, g_recv, t_send, t_recv, c_send, c_recv, i_send, i_recv, p_send, p_recv,
 ):
     blocks, parts, points, antennas, users = chan.shape
@@ -54,27 +54,31 @@
     def ut_flip(mask):
         return (ap, ut_flip_index(mask))
 
+    fetches = [
+        pltpu.make_async_copy(
+            prec_in.at[:, :, :, :, pl.ds(half * width, width)], vbuf.at[0, half], fetch.at[half])
+        for half in range(halves)
+    ]
+    fetches.append(pltpu.make_async_copy(chan_in, chan, fetch.at[halves]))
+    fetches.append(pltpu.make_async_copy(noise_in, noise, fetch.at[halves + 1]))
+    for copy in fetches:
+        copy.start()
+
     barrier = pltpu.get_barrier_semaphore()
     for step in range(1, n_ap):
         pl.semaphore_signal(barrier, inc=1, device_id=ap_peer(step), device_id_type=MESH)
     for mask in range(1, n_ut):
         pl.semaphore_signal(barrier, inc=1, device_id=ut_flip(mask), device_id_type=MESH)
+    for half in range(halves):
+        fetches[half].wait()
     pl.semaphore_wait(barrier, n_ap + n_ut - 2)
 
     pending = []
 
-    def lanes(half):
-        return pl.ds(half * width, width)
-
     def v_copy(mask, half):
-        source = mask ^ low_bit(mask)
-        if source == 0:
-            src = prec.at[:, :, :, :, lanes(half)]
-        else:
-            src = vbuf.at[source - 1, :, :, :, :, lanes(half)]
         return pltpu.make_async_remote_copy(
-            src_ref=src,
-            dst_ref=vbuf.at[mask - 1, :, :, :, :, lanes(half)],
+            src_ref=vbuf.at[mask ^ low_bit(mask), half],
+            dst_ref=vbuf.at[mask, half],
             send_sem=v_send.at[mask - 1, half],
             recv_sem=v_recv.at[mask - 1, half],
             device_id=ut_flip(low_bit(mask)),
@@ -97,7 +101,9 @@
             if later != low_bit(later) and (later ^ low_bit(later)) == mask:
                 v_start(later, half)
 
-    tile_users = users // clus.shape[1]
+    fetches[halves].wait()
+    tiles = clus.shape[0] // points
+    tile_users = users // tiles
     for s in range(blocks):
         turned = []
         for part in range(parts):
@@ -105,8 +111,8 @@
             for a in range(points):
                 value = chan[s, part, a].astype(F32)
                 cut = [
-                    value[:, c * tile_users:(c + 1) * tile_users] * clus[a, c].astype(F32)
-                    for c in range(clus.shape[1])
+                    value[:, c * tile_users:(c + 1) * tile_users] * clus[a * tiles + c].astype(F32)
+                    for c in range(tiles)
                 ]
                 value = cut[0] if len(cut) == 1 else jnp.concatenate(cut, axis=1)
                 point_rows.append(value)
@@ -123,13 +129,17 @@
     all_rows = blocks * 2 * users
     own_bit = [lax.div(ap, 1 << b) % 2 for b in range(bits)]
 
+    def order(c):
+        swapped = bits > 1 and c < lead and c % 2 == 1
+        return [1, 0] + list(range(2, bits)) if swapped else list(range(bits))
+
     def g_copy(level, c):
         return pltpu.make_async_remote_copy(
             src_ref=send[level].at[c],
             dst_ref=recv[level].at[c],
             send_sem=g_send.at[level, c],
             recv_sem=g_recv.at[level, c],
-            device_id=ap_flip(level),
+            device_id=ap_flip(order(c)[level]),
             device_id_type=MESH,
         )
 
@@ -140,21 +150,31 @@
 
     some = blocks // 2
 
-    def gains(s, slot, half):
-        ref = prec if slot == 0 else vbuf.at[slot - 1]
-        field = ref[s, :, :, :, half * width:(half + 1) * width].reshape(2 * rows, width)
-        return jnp.dot(lhs[s], field, preferred_element_type=F32)
+    def gains(s, span, slot, half):
+        field = vbuf[slot, half, s].reshape(2 * rows, width)
+        return jnp.dot(lhs[s, span], field, preferred_element_type=F32)
+
+    def half_rows(c, first, bit):
+        slot, half = chunks[c]
+        if first == 0:
+            return [gains(bit * some + i, slice(None), slot, half) for i in range(some)]
+        span = pl.ds(pl.multiple_of(bit * users, users), users)
+        return [gains(s, span, slot, half) for s in range(blocks)]
 
     def first_stage(c):
         slot, half = chunks[c]
         if slot:
             v_arrived(slot, half)
-        for i in range(some):
-            value = gains((1 - own_bit[0]) * some + i, slot, half)
-            send[0][c, i * 2 * users:(i + 1) * 2 * users] = value.astype(BF16)
+        first = order(c)[0]
+        at = 0
+        for value in half_rows(c, first, 1 - own_bit[first]):
+            send[0][c, at:at + value.shape[0]] = value.astype(BF16)
+            at += value.shape[0]
         g_start(0, c)
-        for i in range(some):
-            keep[0][c, i * 2 * users:(i + 1) * 2 * users] = gains(own_bit[0] * some + i, slot, half)
+        at = 0
+        for value in half_rows(c, first, own_bit[first]):
+            keep[0][c, at:at + value.shape[0]] = value
+            at += value.shape[0]
 
     def next_stage(level, c):
         g_copy(level - 1, c).wait_recv()
@@ -163,8 +183,9 @@
             square[...] = total * total if c == 0 else square[...] + total * total
             return
         size = all_rows >> (level + 1)
-        away = pl.ds(pl.multiple_of((1 - own_bit[level]) * size, size), size)
-        mine = pl.ds(pl.multiple_of(own_bit[level] * size, size), size)
+        bit = own_bit[order(c)[level]]
+        away = pl.ds(pl.multiple_of((1 - bit) * size, size), size)
+        mine = pl.ds(pl.multiple_of(bit * size, size), size)
         send[level][c] = (keep[level - 1][c, away] + recv[level - 1][c, away].astype(F32)).astype(BF16)
         g_start(level, c)
         keep[level][c] = keep[level - 1][c, mine] + recv[level - 1][c, mine].astype(F32)
@@ -181,8 +202,8 @@
         for a in range(points):
             hr = pair[s, a, 0:antennas, 0:users].astype(F32)
             hi = pair[s, a, antennas:2 * antennas, 0:users].astype(F32)
-            vr = prec[s, 0, a].astype(F32)
-            vi = prec[s, 1, a].astype(F32)
+            vr = jnp.concatenate([vbuf[0, h, s, 0, a] for h in range(halves)], axis=1).astype(F32)
+            vi = jnp.concatenate([vbuf[0, h, s, 1, a] for h in range(halves)], axis=1).astype(F32)
             sums[0] = sums[0] + jnp.sum(hr * vr + hi * vi, axis=0, keepdims=True)
             sums[1] = sums[1] + jnp.sum(hr * vi - hi * vr, axis=0, keepdims=True)
         for part in range(2):
@@ -232,6 +253,7 @@
     total = sums[0:blocks]
     signal_re = sums[blocks:2 * blocks]
     signal_im = sums[2 * blocks:3 * blocks]
+    fetches[halves + 1].wait()
     level = total + noise[...]
     strength = signal_re * signal_re + signal_im * signal_im
     weight = level / (level - strength)
@@ -285,26 +307,42 @@
 
     sign = jnp.where(lane_row < antennas, -1.0, 1.0).astype(F32)
 
-    def sweep(k, carry):
-        is_row = row_of == k
-        at_re = lane_of == k
-        at_im = lane_of == k + antennas
-        clear = is_row | at_re | at_im
+    def pick(row, lane):
+        return jnp.sum(jnp.where(lane_of[0:row.shape[0]] == lane, row, 0.0), axis=1, keepdims=True)
+
+    def sweep(pair_index, carry):
+        k = pair_index * 2
+        lane = jnp.where(lane_row >= antennas, lane_row - antennas, lane_row)
+        in_pair = (lane == k) | (lane == k + 1)
+        is_first = row_of == k
+        is_second = row_of == k + 1
+        clear = is_first | is_second | in_pair
         for p in range(per):
             value = work[p]
-            row = work[p, pl.ds(k, 1)]
-            pivot = jnp.sum(jnp.where(lane_row == k, row, 0.0), axis=1, keepdims=True)
-            inverse = 1.0 / pivot
-            col_re = jnp.sum(jnp.where(at_re, value, 0.0), axis=1, keepdims=True)
-            col_im = jnp.sum(jnp.where(at_im, value, 0.0), axis=1, keepdims=True)
-            row = jnp.where(lane_row == k, -inverse, jnp.where(lane_row == k + antennas, 0.0, row * inverse))
-            turned = pltpu.roll(row, antennas, 1) * sign
-            col_re = jnp.where(is_row, -1.0, col_re)
-            col_im = jnp.where(is_row, 0.0, col_im)
-            work[p] = jnp.where(clear, 0.0, value) - (col_re * row + col_im * turned)
+            row1 = work[p, pl.ds(k, 1)]
+            row2 = work[p, pl.ds(k + 1, 1)]
+            d1 = pick(row1, k)
+            d2 = pick(row2, k + 1)
+            gr = pick(row1, k + 1)
+            gn = pick(row1, antennas + k + 1)
+            q = 1.0 / (d1 * d2 - (gr * gr + gn * gn))
+            d1, d2, gr, gn = d1 * q, d2 * q, gr * q, gn * q
+            r1 = jnp.where(in_pair, jnp.where(lane_row == k, -1.0, 0.0), row1)
+            r2 = jnp.where(in_pair, jnp.where(lane_row == k + 1, -1.0, 0.0), row2)
+            t1 = pltpu.roll(r1, antennas, 1) * sign
+            t2 = pltpu.roll(r2, antennas, 1) * sign
+            p1 = d2 * r1 - (gr * r2 + gn * t2)
+            tp1 = d2 * t1 - (gr * t2 - gn * r2)
+            p2 = d1 * r2 - (gr * r1 - gn * t1)
+            tp2 = d1 * t2 - (gr * t1 + gn * r1)
+            c1r = jnp.where(is_first, -1.0, jnp.where(is_second, 0.0, pick(value, k)))
+            c1n = jnp.where(is_first | is_second, 0.0, pick(value, antennas + k))
+            c2r = jnp.where(is_second, -1.0, jnp.where(is_first, 0.0, pick(value, k + 1)))
+            c2n = jnp.where(is_first | is_second, 0.0, pick(value, antennas + k + 1))
+            work[p] = jnp.where(clear, 0.0, value) - ((c1r * p1 + c1n * tp1) + (c2r * p2 + c2n * tp2))
         return carry
 
-    lax.fori_loop(0, antennas, sweep, 0)
+    lax.fori_loop(0, antennas // 2, sweep, 0)
     for p in range(per):
         invs[ut, p] = -work[p]
 
@@ -381,6 +419,7 @@
     sizes = [all_rows >> (b + 1) for b in range(bits)]
     vmem = pl.BlockSpec(memory_space=pltpu.VMEM)
     smem = pl.BlockSpec(memory_space=pltpu.SMEM)
+    hbm = pl.BlockSpec(memory_space=pl.ANY)
     dma = pltpu.SemaphoreType.DMA
     return pl.pallas_call(
         functools.partial(kernel, n_ap, n_ut, bits, width),
@@ -388,10 +427,13 @@
             jax.ShapeDtypeStruct(channel.shape, BF16),
             jax.ShapeDtypeStruct((blocks, users), F32),
         ),
-        in_specs=[vmem, vmem, smem, vmem, smem, smem],
+        in_specs=[hbm, hbm, smem, hbm, smem, smem],
         out_specs=(vmem, vmem),
         scratch_shapes=[
-            pltpu.VMEM((n_ut - 1,) + channel.shape, BF16),
+            pltpu.VMEM(channel.shape, BF16),
+            pltpu.VMEM(noise.shape, F32),
+            dma((halves + 2,)),
+            pltpu.VMEM((n_ut, halves) + channel.shape[:-1] + (width,), BF16),
             pltpu.VMEM((blocks, 2 * users, 2 * rows), BF16),
             pltpu.VMEM((blocks, points, 2 * antennas, 2 * users), BF16),
             [pltpu.VMEM((count, size, width), BF16) for size in sizes],
@@ -419,9 +461,9 @@
             dma((n_ut - 1,)),
         ],
         compiler_params=pltpu.CompilerParams(
-            collective_id=0, has_side_effects=True, vmem_limit_bytes=40 * 1024 * 1024
+            collective_id=0, has_side_effects=True, vmem_limit_bytes=56 * 1024 * 1024
         ),
-    )(channel, start_precoder, cluster, noise, penalty, power)
+    )(channel, start_precoder, cluster.reshape(-1), noise, penalty, power)
 
 
 def solution(mesh):

time: 83.5 us -> 70.8 us (0.85)
  Pallas kernels: 77.7 us -> 67.6 us
  local copies, waits for them, and re-layouts: 4.87 us -> 2.46 us
    pallas_call x1, Pallas kernels: 77.7 us -> 67.6 us  [local(): pl.pallas_call(functools.partial(kernel, n_ap, n_ut, bits, width), out_sh...]
    unnamed x13 -> x4, local copies, waits for them, and re-layouts: 4.87 us -> 2.46 us
where the time goes in v2:
time: 70.8 us; the launch traced here: 70.7 us
  Pallas kernels  67.6 us (95%)
  local copies, waits for them, and re-layouts  2.46 us (3%)
    pallas_call x1, Pallas kernels, local(): pl.pallas_call(functools.partial(kernel, n_ap, n_ut, bits, width), out_sh...  67.6 us
    unnamed x4, local copies, waits for them, and re-layouts  2.46 us

profile of v2, /device:TPU:0, one launch (start us, length us, event | category | flops | bytes accessed | tf_op | source)
XLA Modules:
  0.0 70.7 jit_solution(2075468781772163549)
XLA Ops:
  0.6 67.6 %shard_map.77 = (bf16[2,2,4,64,256]{4,3,2,1,0:T(8,128)(2,1)}, f32[2,256]{1,0:T(2,128)}) custom-call(bf16[2,2,4,64,256]{4,3,2,1,0:T(8,128)(2,1)} %chan_in.1, bf16[2,2,4,64,256]{4,3,2,1,0:T(8,128)(2,1)} %prec_in.1, s32[4]{0:T(128)} %bitcast.1, f32[2,256]{1,0:T(2,128)} %noise_in.1, f32[4]{0:T(128)} %penalty.1, f32[4]{0:T(128)} %power.1), custom_call_target="tpu_custom_call" | custom-call | tf_op jit(solution)/shard_map/pallas_call | solution.py:424
  68.2 0.0 copy-start
  68.2 1.9 %copy.10 = bf16[2,2,4,64,256]{4,3,2,1,0:T(8,128)(2,1)} copy(bf16[2,2,4,64,256]{4,3,2,1,0:T(8,128)(2,1)} %get-tuple-element.4) | data formatting | bytes 1048576
  70.1 0.0 copy-done
  70.1 0.6 copy.11
Async XLA Ops:
  68.2 1.9 %copy-start = (f32[2,256]{1,0:T(2,128)S(1)}, f32[2,256]{1,0:T(2,128)}, u32[]{:S(2)}) copy-start(f32[2,256]{1,0:T(2,128)} %get-tuple-element.5) | copy-start | bytes 6148

commit v3 on v2

--- a/solution.py
+++ b/solution.py
@@ -130,7 +130,7 @@
     own_bit = [lax.div(ap, 1 << b) % 2 for b in range(bits)]
 
     def order(c):
-        swapped = bits > 1 and c < lead and c % 2 == 1
+        swapped = bits > 1 and c >= lead and (c - lead) % 2 == 1
         return [1, 0] + list(range(2, bits)) if swapped else list(range(bits))
 
     def g_copy(level, c):
@@ -209,11 +209,12 @@
         for part in range(2):
             msgs[ap, blocks * (1 + part) + s:blocks * (1 + part) + s + 1] = sums[part]
 
+    turn = sorted(range(count), key=lambda c: c if c < lead or (c - lead) % 2 == 0 else c - 1.5)
     for i in range(count + bits - 1):
         for level in range(1, bits + 1):
-            c = i - (level - 1)
-            if 0 <= c < count:
-                next_stage(level, c)
+            at = i - (level - 1)
+            if 0 <= at < count:
+                next_stage(level, turn[at])
         if lead + i < count:
             first_stage(lead + i)
 
@@ -342,7 +343,7 @@
             work[p] = jnp.where(clear, 0.0, value) - ((c1r * p1 + c1n * tp1) + (c2r * p2 + c2n * tp2))
         return carry
 
-    lax.fori_loop(0, antennas // 2, sweep, 0)
+    lax.fori_loop(0, antennas // 2, sweep, 0, unroll=2)
     for p in range(per):
         invs[ut, p] = -work[p]
 

time: 70.8 us -> 70.1 us (level)
  Pallas kernels: 67.6 us -> 66.8 us
    pallas_call x1, Pallas kernels: 67.6 us -> 66.8 us  [local(): pl.pallas_call(functools.partial(kernel, n_ap, n_ut, bits, width), out_sh...]
where the time goes in v3:
time: 70.1 us; the launch traced here: 69.9 us
  Pallas kernels  66.8 us (95%)
  local copies, waits for them, and re-layouts  2.46 us (4%)
    pallas_call x1, Pallas kernels, local(): pl.pallas_call(functools.partial(kernel, n_ap, n_ut, bits, width), out_sh...  66.8 us
    unnamed x4, local copies, waits for them, and re-layouts  2.46 us

profile of v3, /device:TPU:0, one launch (start us, length us, event | category | flops | bytes accessed | tf_op | source)
XLA Modules:
  0.0 69.9 jit_solution(8887874117631996552)
XLA Ops:
  0.6 66.8 %shard_map.77 = (bf16[2,2,4,64,256]{4,3,2,1,0:T(8,128)(2,1)}, f32[2,256]{1,0:T(2,128)}) custom-call(bf16[2,2,4,64,256]{4,3,2,1,0:T(8,128)(2,1)} %chan_in.1, bf16[2,2,4,64,256]{4,3,2,1,0:T(8,128)(2,1)} %prec_in.1, s32[4]{0:T(128)} %bitcast.1, f32[2,256]{1,0:T(2,128)} %noise_in.1, f32[4]{0:T(128)} %penalty.1, f32[4]{0:T(128)} %power.1), custom_call_target="tpu_custom_call" | custom-call | tf_op jit(solution)/shard_map/pallas_call | solution.py:425
  67.4 0.0 copy-start
  67.4 1.9 %copy.10 = bf16[2,2,4,64,256]{4,3,2,1,0:T(8,128)(2,1)} copy(bf16[2,2,4,64,256]{4,3,2,1,0:T(8,128)(2,1)} %get-tuple-element.4) | data formatting | bytes 1048576
  69.3 0.0 copy-done
  69.3 0.6 copy.11
Async XLA Ops:
  67.4 1.9 %copy-start = (f32[2,256]{1,0:T(2,128)S(1)}, f32[2,256]{1,0:T(2,128)}, u32[]{:S(2)}) copy-start(f32[2,256]{1,0:T(2,128)} %get-tuple-element.5) | copy-start | bytes 6148
